TPU v7x, 32 devices: a whole 2x2x4 slice. The times are simulated.
32 devices in a mesh: groups: 2 (over y), mesh: 4 (over z), grid: 2 (over x), mp: 2 (over core).
Axes of the slice: x: 2, y: 2, z: 4, core: 2. Of those that a mesh axis runs over, the one named last changes fastest.
Arguments:
- grid_latent: bfloat16 [4096, 512], P(('groups', 'mesh', 'grid'), 'mp'), parts along dimension 0, may hold values from -6 to 6
- mesh_latent: bfloat16 [8192, 512], P(('groups', 'mesh', 'grid'), 'mp'), parts along dimension 0, may hold values from -6 to 6
- local_targets: int32 [2048, 3], P(('mesh', 'grid')), may hold values from 0 to 511
- grid_slots: int32 [32, 32], P(('mesh', 'grid')), may hold values from 0 to 255
- mesh_slots: int32 [32, 32], P(('mesh', 'grid')), may hold values from -1 to 511, as said below
- mesh_links: int32 [4096, 6], P(('mesh', 'grid')), may hold values from 0 to 1535
- encode_in: bfloat16 [512, 512], P(None, 'mp'), may hold values from -0.25 to 0.25
- encode_out: bfloat16 [512, 512], P('mp'), may hold values from -0.25 to 0.25
- process_in: bfloat16 [512, 512], P(None, 'mp'), may hold values from -0.25 to 0.25
- process_out: bfloat16 [512, 512], P('mp'), may hold values from -0.25 to 0.25
- decode_in: bfloat16 [512, 512], P(None, 'mp'), may hold values from -0.25 to 0.25
- decode_out: bfloat16 [512, 512], P('mp'), may hold values from -0.25 to 0.25
- cotangent: bfloat16 [4096, 512], P(('groups', 'mesh', 'grid'), 'mp'), parts along dimension 0, may hold values from -0.0625 to 0.0625
Outputs:
- prediction: bfloat16 [4096, 512], P(('groups', 'mesh', 'grid'), 'mp'), parts along dimension 0
- grad_up: float32 [1024, 512], P('groups', 'mp'), parts along dimension 0
- grad_down: float32 [1024, 512], P(('groups', 'mp')), parts along dimension 0
There are 2 independent parts, one for each index of `groups`. A program takes and returns all parts, laid end to end along the dimension named above; an argument that names none is the same for every part. Nothing has to cross between parts.
Inputs may be any that keep to these rules, and one draw needn't show every extreme that they name: `mesh_slots`: within each row the slots in use come first, 16 of them or more; one partition receives all 32 slots from each of its four nearest partitions.
All inputs are finite; a program needn't handle non-finite values.
Results may differ from a plain program's by a relative error of at most 0.0085.
Values may be sent and summed in bfloat16 or wider, within the bound.
A program may use at most 64 MiB of HBM per device.

v0:
```python
import jax
import jax.numpy as jnp
from jax import lax
from jax.sharding import PartitionSpec as P

slot_offsets = (-2, -1, 1, 2)


def passed_along(shard, axis, by):
    devices = lax.axis_size(axis)
    return lax.ppermute(shard, axis, [(i, (i + by) % devices) for i in range(devices)])


def with_halo(shard, sides, width):
    for axis, dim in sides:
        devices, length = (lax.axis_size(axis), shard.shape[dim])
        up = [(i, (i + 1) % devices) for i in range(devices)]
        down = [(j, i) for i, j in up]
        last = lax.slice_in_dim(shard, length - width, length, axis=dim)
        initial = lax.slice_in_dim(shard, 0, width, axis=dim)
        before = lax.ppermute(last, axis, up)
        after = lax.ppermute(initial, axis, down)
        shard = jnp.concatenate([before, shard, after], axis=dim)
    return shard


def widen(values):
    return lax.all_gather(values, "mp", axis=1, tiled=True)


def mlp_block(values, weight_in, weight_out):
    widened = widen(values.astype(jnp.bfloat16)).astype(jnp.float32)
    center = widened - jnp.mean(widened, axis=-1, keepdims=True)
    spread = jnp.mean(center * center, axis=-1, keepdims=True)
    normed = (center * lax.rsqrt(spread + 1e-05)).astype(jnp.bfloat16)
    before = jnp.dot(normed, weight_in, preferred_element_type=jnp.float32)
    activated = jax.nn.silu(before).astype(jnp.bfloat16)
    partial_sum = jnp.dot(activated, weight_out, preferred_element_type=jnp.float32)
    result = lax.psum_scatter(partial_sum, "mp", scatter_dimension=1, tiled=True)
    return (result, normed, before, activated)


def route(buffer):
    pieces = []
    for which in range(4):
        pieces.append(passed_along(buffer[which], ("mesh", "grid"), slot_offsets[which]))
    return jnp.stack(pieces, axis=0)


def on_device(
    grid_latent,
    mesh_latent,
    local_targets,
    grid_slots,
    mesh_slots,
    mesh_links,
    encode_in,
    encode_out,
    process_in,
    process_out,
    decode_in,
    decode_out,
    cotangent,
):
    grid_rows = grid_latent.shape[0]
    mesh_rows = mesh_latent.shape[0]
    half_width = grid_latent.shape[1]
    capacity = grid_slots.shape[1]
    contract_first = (((0,), (0,)), ((), ()))
    mesh_range = jnp.arange(mesh_rows, dtype=jnp.int32)
    local_counts = jnp.zeros((mesh_rows, grid_rows), jnp.float32)
    for column in range(local_targets.shape[1]):
        local_counts = local_counts + (
            mesh_range[:, None] == local_targets[:, column][None, :]
        ).astype(jnp.float32)
    local_counts = local_counts.astype(jnp.bfloat16)
    picker = (
        grid_slots.reshape(-1)[:, None] == jnp.arange(grid_rows, dtype=jnp.int32)[None, :]
    ).astype(jnp.bfloat16)
    placer = (mesh_range[:, None] == mesh_slots.reshape(-1)[None, :]).astype(jnp.bfloat16)
    outgoing = jnp.dot(picker, grid_latent, preferred_element_type=jnp.float32).astype(jnp.bfloat16)
    arrived = route(outgoing.reshape(4, capacity, half_width)).reshape(4 * capacity, half_width)
    mesh_sum = jnp.dot(placer, arrived, preferred_element_type=jnp.float32) + jnp.dot(
        local_counts, grid_latent, preferred_element_type=jnp.float32
    )
    encoded = mlp_block(mesh_sum, encode_in, encode_out)[0]
    mesh_state = (mesh_latent + encoded).astype(jnp.bfloat16)
    padded = with_halo(mesh_state, ((("mesh", "grid"), 0),), mesh_rows)
    window = jnp.arange(3 * mesh_rows, dtype=jnp.int32)
    counts = jnp.zeros((mesh_rows, 3 * mesh_rows), jnp.float32)
    for column in range(mesh_links.shape[1]):
        counts = counts + (mesh_links[:, column][:, None] == window[None, :]).astype(jnp.float32)
    gathered = jnp.dot(counts.astype(jnp.bfloat16), padded, preferred_element_type=jnp.float32)
    processed = mlp_block(gathered, process_in, process_out)[0]
    mesh_final = (mesh_state + processed).astype(jnp.bfloat16)
    returning = lax.dot_general(
        placer, mesh_final, contract_first, preferred_element_type=jnp.float32
    ).astype(jnp.bfloat16)
    reversed_back = route(returning.reshape(4, capacity, half_width)[::-1])[::-1]
    landed = reversed_back.reshape(4 * capacity, half_width)
    grid_sum = lax.dot_general(
        picker, landed, contract_first, preferred_element_type=jnp.float32
    ) + lax.dot_general(
        local_counts, mesh_final, contract_first, preferred_element_type=jnp.float32
    )
    decoded, normed, before, activated = mlp_block(grid_sum, decode_in, decode_out)
    prediction = (grid_latent + decoded).astype(jnp.bfloat16)
    upstream = widen(cotangent)
    down_part = lax.dot_general(
        activated, upstream, contract_first, preferred_element_type=jnp.float32
    )
    hidden_grad = lax.dot_general(
        upstream, decode_out, (((1,), (1,)), ((), ())), preferred_element_type=jnp.float32
    )
    gate_value = jax.nn.sigmoid(before)
    before_grad = (hidden_grad * gate_value * (1.0 + before * (1.0 - gate_value))).astype(
        jnp.bfloat16
    )
    up_part = lax.dot_general(
        normed, before_grad, contract_first, preferred_element_type=jnp.float32
    )
    grad_up, grad_down = lax.psum((up_part, down_part), ("mesh", "grid"))
    return (prediction, grad_up, grad_down)


def solution(mesh):
    placed = (
        P(("groups", "mesh", "grid"), "mp"),
        P(("groups", "mesh", "grid"), "mp"),
        P(("mesh", "grid"), None),
        P(("mesh", "grid"), None),
        P(("mesh", "grid"), None),
        P(("mesh", "grid"), None),
        P(None, "mp"),
        P("mp", None),
        P(None, "mp"),
        P("mp", None),
        P(None, "mp"),
        P("mp", None),
        P(("groups", "mesh", "grid"), "mp"),
    )
    return jax.shard_map(
        on_device,
        mesh=mesh,
        in_specs=placed,
        out_specs=(
            P(("groups", "mesh", "grid"), "mp"),
            P("groups", "mp"),
            P(("groups", "mp"), None),
        ),
        check_vma=False,
    )
```

profile of v0, /device:TPU:0, one launch (start us, length us, event | category | flops | bytes accessed | tf_op | source)
XLA Modules:
  0.0 183.1 jit_solution(12175643167793850891)
XLA Ops:
  9.2 3.1 %collective-permute-start.3 = (bf16[32,256]{1,0:T(8,128)(2,1)S(1)}, bf16[32,256]{1,0:T(8,128)(2,1)S(1)}, u32[]{:S(2)}, u32[]{:S(2)}) collective-permute-start(bf16[32,256]{1,0:T(8,128)(2,1)S(1)} %get-tuple-element.10), channel_id=1, source_target_pairs={{0,4},{2,6},{4,8},{6,10},{8,12},{10,14},{12,0},{14,2},{1,5},{3,7},... | collective-permute-start | bytes 49160 | tf_op jit(solution)/shard_map/ppermute | solution.py:11
  12.2 1.5 collective-permute-start.2
  13.7 3.2 %collective-permute-start.1 = (bf16[32,256]{1,0:T(8,128)(2,1)S(1)}, bf16[32,256]{1,0:T(8,128)(2,1)S(1)}, u32[]{:S(2)}, u32[]{:S(2)}) collective-permute-start(bf16[32,256]{1,0:T(8,128)(2,1)S(1)} %get-tuple-element.12), channel_id=1, source_target_pairs={{0,14},{2,0},{4,2},{6,4},{8,6},{10,8},{12,10},{14,12},{1,15},{3,1}... | collective-permute-start | bytes 49160 | tf_op jit(solution)/shard_map/ppermute | solution.py:11
  20.9 2.3 %all_gather.12 = bf16[512,512]{1,0:T(8,128)(2,1)S(1)} all-gather(bf16[512,256]{1,0:T(8,128)(2,1)S(1)} %fusion.11), channel_id=1, replica_groups=mesh['groups'=2,'mesh'=4,'grid'=2,'mp'=2] {'mp'}, dimensions={1}, use_global_device_ids=true | all-gather | bytes 786432 | tf_op jit(solution)/shard_map/all_gather | solution.py:28
  23.8 1.7 fusion.46
  25.5 8.1 %reduce-scatter.4.cloned.1.call-done = f32[512,256]{1,0:T(8,128)} async-done(((f32[512,512]{1,0:T(8,128)}), f32[512,256]{1,0:T(8,128)}) %reduce-scatter.4.cloned.1.call-update) | async-done | bytes 524304 | tf_op jit(solution)/shard_map/reduce_scatter | solution.py:39
  34.7 4.5 %collective-permute-start.5 = (bf16[512,256]{1,0:T(8,128)(2,1)S(1)}, bf16[512,256]{1,0:T(8,128)(2,1)S(1)}, u32[]{:S(2)}, u32[]{:S(2)}) collective-permute-start(bf16[512,256]{1,0:T(8,128)(2,1)S(1)} %add_convert_fusion.5), channel_id=1, source_target_pairs={{2,0},{4,2},{6,4},{8,6},{10,8},{12,10},{14,12},{0,14},{3,1},{5,3},... | collective-permute-start | bytes 786440 | tf_op jit(solution)/shard_map/ppermute | solution.py:22
  39.3 6.0 %collective-permute-done.5 = bf16[512,256]{1,0:T(8,128)(2,1)S(1)} collective-permute-done((bf16[512,256]{1,0:T(8,128)(2,1)S(1)}, bf16[512,256]{1,0:T(8,128)(2,1)S(1)}, u32[]{:S(2)}, u32[]{:S(2)}) %collective-permute-start.5) | collective-permute-done | bytes 262176 | tf_op jit(solution)/shard_map/ppermute | solution.py:22
  45.3 4.9 %collective-permute-done.4 = bf16[512,256]{1,0:T(8,128)(2,1)S(1)} collective-permute-done((bf16[512,256]{1,0:T(8,128)(2,1)S(1)}, bf16[512,256]{1,0:T(8,128)(2,1)S(1)}, u32[]{:S(2)}, u32[]{:S(2)}) %collective-permute-start.4) | collective-permute-done | bytes 262176 | tf_op jit(solution)/shard_map/ppermute | solution.py:21
  50.2 2.5 %fusion.12 = bf16[512,256]{1,0:T(8,128)(2,1)S(1)} fusion(s32[512]{0:T(512)S(1)} %bitcast.46, s32[512]{0:T(512)S(1)} %bitcast.47, s32[512]{0:T(512)S(1)} %bitcast.43, s32[512]{0:T(512)S(1)} %bitcast.44, s32[512]{0:T(512)S(1)} %bitcast.45, s32[512]{0:T(512)S(1)} %bitcast.42, bf16[512,256]{1,0:T(8,128)(2,1)S(1)} %collective-permute-done.5, ...), kind=kOutput, calls=%fused_computation.24 | convolution fusion | flops 419299328 | bytes 1060864 | tf_op jit(solution)/shard_map/dot_general | solution.py:93
  52.7 2.3 %all_gather.13 = bf16[512,512]{1,0:T(8,128)(2,1)S(1)} all-gather(bf16[512,256]{1,0:T(8,128)(2,1)S(1)} %fusion.12), channel_id=1, replica_groups=mesh['groups'=2,'mesh'=4,'grid'=2,'mp'=2] {'mp'}, dimensions={1}, use_global_device_ids=true | all-gather | bytes 786432 | tf_op jit(solution)/shard_map/all_gather | solution.py:28
  55.5 1.7 fusion.37
  57.3 8.8 %reduce-scatter.6.cloned.1.call-done = f32[512,256]{1,0:T(8,128)} async-done(((f32[512,512]{1,0:T(8,128)}), f32[512,256]{1,0:T(8,128)}) %reduce-scatter.6.cloned.1.call-update) | async-done | bytes 524304 | tf_op jit(solution)/shard_map/reduce_scatter | solution.py:39
  67.5 1.8 collective-permute-start.9
  69.3 1.5 collective-permute-start.8
  70.7 3.3 %collective-permute-start.7 = (bf16[32,256]{1,0:T(8,128)(2,1)S(1)}, bf16[32,256]{1,0:T(8,128)(2,1)S(1)}, u32[]{:S(2)}, u32[]{:S(2)}) collective-permute-start(bf16[32,256]{1,0:T(8,128)(2,1)S(1)} %get-tuple-element.8), channel_id=1, source_target_pairs={{0,14},{2,0},{4,2},{6,4},{8,6},{10,8},{12,10},{14,12},{1,15},{3,1}... | collective-permute-start | bytes 49160 | tf_op jit(solution)/shard_map/ppermute | solution.py:11
  74.3 1.4 collective-permute-done.8
  75.7 2.0 %collective-permute-done.6 = bf16[32,256]{1,0:T(8,128)(2,1)S(1)} collective-permute-done((bf16[32,256]{1,0:T(8,128)(2,1)S(1)}, bf16[32,256]{1,0:T(8,128)(2,1)S(1)}, u32[]{:S(2)}, u32[]{:S(2)}) %collective-permute-start.6) | collective-permute-done | bytes 16416 | tf_op jit(solution)/shard_map/ppermute | solution.py:11
  78.5 2.1 %all_gather.14 = bf16[256,512]{1,0:T(8,128)(2,1)S(1)} all-gather(bf16[256,256]{1,0:T(8,128)(2,1)S(1)} %fusion.14), channel_id=1, replica_groups=mesh['groups'=2,'mesh'=4,'grid'=2,'mp'=2] {'mp'}, dimensions={1}, use_global_device_ids=true | all-gather | bytes 393216 | tf_op jit(solution)/shard_map/all_gather | solution.py:28
  82.4 2.0 %all_gather.15 = bf16[256,512]{1,0:T(8,128)(2,1)S(1)} all-gather(bf16[256,256]{1,0:T(8,128)(2,1)S(1)} %copy-done.6), channel_id=1, replica_groups=mesh['groups'=2,'mesh'=4,'grid'=2,'mp'=2] {'mp'}, dimensions={1}, use_global_device_ids=true | all-gather | bytes 393216 | tf_op jit(solution)/shard_map/all_gather | solution.py:28
  86.9 2.9 %reduce-scatter.8.cloned.1.call-done = f32[256,256]{1,0:T(8,128)} async-done(((f32[256,512]{1,0:T(8,128)}), f32[256,256]{1,0:T(8,128)}) %reduce-scatter.8.cloned.1.call-update) | async-done | bytes 262160 | tf_op jit(solution)/shard_map/reduce_scatter | solution.py:39
  89.9 1.6 add_convert_fusion.7
  91.5 82.4 %all-reduce.3.cloned.1.call-done = (f32[512,256]{1,0:T(8,128)}, f32[256,512]{1,0:T(8,128)}) async-done(((f32[512,256]{1,0:T(8,128)}, f32[256,512]{1,0:T(8,128)}), (f32[512,256]{1,0:T(8,128)}, f32[256,512]{1,0:T(8,128)})) %all-reduce.3.cloned.1.call-update) | async-done | bytes 1048592 | tf_op jit(solution)/shard_map/psum | solution.py:122
  173.9 1.9 %copy.18 = f32[512,256]{1,0:T(8,128)} copy(f32[512,256]{1,0:T(8,128)} %get-tuple-element.23) | data formatting | bytes 1048576
  (76 shorter events, 15.5 us)
Async XLA Ops:
  7.2 16.6 %copy-start = (bf16[256,512]{1,0:T(8,128)(2,1)S(1)}, bf16[256,512]{1,0:T(8,128)(2,1)}, u32[]{:S(2)}) copy-start(bf16[256,512]{1,0:T(8,128)(2,1)} %param.20) | copy-start | bytes 786436
  7.2 12.1 %copy-start.8 = (s32[4,32]{1,0:T(4,128)S(1)}, s32[4,32]{1,0:T(4,128)}, u32[]{:S(2)}) copy-start(s32[4,32]{1,0:T(4,128)} %param.17) | copy-start | bytes 1540
  7.2 26.4 %reduce-scatter.4.cloned.1.call-start = ((), (), s32[]{:S(2)}) async-start(), calls=%async_computation.3 | async-start | bytes 1572864 | tf_op jit(solution)/shard_map/reduce_scatter | solution.py:39
  9.2 10.2 %collective-permute-start.3 = (bf16[32,256]{1,0:T(8,128)(2,1)S(1)}, bf16[32,256]{1,0:T(8,128)(2,1)S(1)}, u32[]{:S(2)}, u32[]{:S(2)}) collective-permute-start(bf16[32,256]{1,0:T(8,128)(2,1)S(1)} %get-tuple-element.10), channel_id=1, source_target_pairs={{0,4},{2,6},{4,8},{6,10},{8,12},{10,14},{12,0},{14,2},{1,5},{3,7},... | collective-permute-start | bytes 49160 | tf_op jit(solution)/shard_map/ppermute | solution.py:11
  12.2 7.1 %collective-permute-start.2 = (bf16[32,256]{1,0:T(8,128)(2,1)S(1)}, bf16[32,256]{1,0:T(8,128)(2,1)S(1)}, u32[]{:S(2)}, u32[]{:S(2)}) collective-permute-start(bf16[32,256]{1,0:T(8,128)(2,1)S(1)} %get-tuple-element.11), channel_id=1, source_target_pairs={{0,2},{2,4},{4,6},{6,8},{8,10},{10,12},{12,14},{14,0},{1,3},{3,5},... | collective-permute-start | bytes 49160 | tf_op jit(solution)/shard_map/ppermute | solution.py:11
  13.7 5.6 %collective-permute-start.1 = (bf16[32,256]{1,0:T(8,128)(2,1)S(1)}, bf16[32,256]{1,0:T(8,128)(2,1)S(1)}, u32[]{:S(2)}, u32[]{:S(2)}) collective-permute-start(bf16[32,256]{1,0:T(8,128)(2,1)S(1)} %get-tuple-element.12), channel_id=1, source_target_pairs={{0,14},{2,0},{4,2},{6,4},{8,6},{10,8},{12,10},{14,12},{1,15},{3,1}... | collective-permute-start | bytes 49160 | tf_op jit(solution)/shard_map/ppermute | solution.py:11
  17.0 3.7 %collective-permute-start = (bf16[32,256]{1,0:T(8,128)(2,1)S(1)}, bf16[32,256]{1,0:T(8,128)(2,1)S(1)}, u32[]{:S(2)}, u32[]{:S(2)}) collective-permute-start(bf16[32,256]{1,0:T(8,128)(2,1)S(1)} %get-tuple-element.9), channel_id=1, source_target_pairs={{0,12},{2,14},{4,0},{6,2},{8,4},{10,6},{12,8},{14,10},{1,13},{3,15... | collective-permute-start | bytes 49160 | tf_op jit(solution)/shard_map/ppermute | solution.py:11
  20.9 2.8 %copy-start.9 = (bf16[512,256]{1,0:T(8,128)(2,1)S(1)}, bf16[512,256]{1,0:T(8,128)(2,1)}, u32[]{:S(2)}) copy-start(bf16[512,256]{1,0:T(8,128)(2,1)} %param.19) | copy-start | bytes 786436
  25.5 8.2 %copy-start.5 = (bf16[512,256]{1,0:T(8,128)(2,1)S(1)}, bf16[512,256]{1,0:T(8,128)(2,1)}, u32[]{:S(2)}) copy-start(bf16[512,256]{1,0:T(8,128)(2,1)} %param.14) | copy-start | bytes 786436
  25.5 13.8 %copy-start.7 = (s32[512,6]{0,1:T(8,128)S(1)}, s32[512,6]{0,1:T(8,128)}, u32[]{:S(2)}) copy-start(s32[512,6]{0,1:T(8,128)} %param.18) | copy-start | bytes 36868
  25.5 40.6 %reduce-scatter.6.cloned.1.call-start = ((), (), s32[]{:S(2)}) async-start(), calls=%async_computation.4 | async-start | bytes 1572864 | tf_op jit(solution)/shard_map/reduce_scatter | solution.py:39
  34.7 10.6 %collective-permute-start.5 = (bf16[512,256]{1,0:T(8,128)(2,1)S(1)}, bf16[512,256]{1,0:T(8,128)(2,1)S(1)}, u32[]{:S(2)}, u32[]{:S(2)}) collective-permute-start(bf16[512,256]{1,0:T(8,128)(2,1)S(1)} %add_convert_fusion.5), channel_id=1, source_target_pairs={{2,0},{4,2},{6,4},{8,6},{10,8},{12,10},{14,12},{0,14},{3,1},{5,3},... | collective-permute-start | bytes 786440 | tf_op jit(solution)/shard_map/ppermute | solution.py:22
  39.2 11.0 %collective-permute-start.4 = (bf16[512,256]{1,0:T(8,128)(2,1)S(1)}, bf16[512,256]{1,0:T(8,128)(2,1)S(1)}, u32[]{:S(2)}, u32[]{:S(2)}) collective-permute-start(bf16[512,256]{1,0:T(8,128)(2,1)S(1)} %add_convert_fusion.5), channel_id=1, source_target_pairs={{0,2},{2,4},{4,6},{6,8},{8,10},{10,12},{12,14},{14,0},{1,3},{3,5},... | collective-permute-start | bytes 786440 | tf_op jit(solution)/shard_map/ppermute | solution.py:21
  52.7 2.8 %copy-start.10 = (bf16[256,512]{1,0:T(8,128)(2,1)S(1)}, bf16[256,512]{1,0:T(8,128)(2,1)}, u32[]{:S(2)}) copy-start(bf16[256,512]{1,0:T(8,128)(2,1)} %param.22) | copy-start | bytes 786436
  52.7 2.8 %copy-start.11 = (bf16[512,256]{1,0:T(8,128)(2,1)S(1)}, bf16[512,256]{1,0:T(8,128)(2,1)}, u32[]{:S(2)}) copy-start(bf16[512,256]{1,0:T(8,128)(2,1)} %param.21) | copy-start | bytes 786436
  57.3 32.6 %reduce-scatter.8.cloned.1.call-start = ((), (), s32[]{:S(2)}) async-start(), calls=%async_computation.5 | async-start | bytes 786432 | tf_op jit(solution)/shard_map/reduce_scatter | solution.py:39
  66.1 12.0 %copy-start.1 = (f32[512,256]{1,0:T(8,128)S(1)}, f32[512,256]{1,0:T(8,128)}, u32[]{:S(2)}) copy-start(f32[512,256]{1,0:T(8,128)} %reduce-scatter.6.cloned.1.call-done) | copy-start | bytes 1572868
  67.5 6.8 %collective-permute-start.9 = (bf16[32,256]{1,0:T(8,128)(2,1)S(1)}, bf16[32,256]{1,0:T(8,128)(2,1)S(1)}, u32[]{:S(2)}, u32[]{:S(2)}) collective-permute-start(bf16[32,256]{1,0:T(8,128)(2,1)S(1)} %get-tuple-element.6), channel_id=1, source_target_pairs={{0,4},{2,6},{4,8},{6,10},{8,12},{10,14},{12,0},{14,2},{1,5},{3,7},... | collective-permute-start | bytes 49160 | tf_op jit(solution)/shard_map/ppermute | solution.py:11
  69.3 6.4 %collective-permute-start.8 = (bf16[32,256]{1,0:T(8,128)(2,1)S(1)}, bf16[32,256]{1,0:T(8,128)(2,1)S(1)}, u32[]{:S(2)}, u32[]{:S(2)}) collective-permute-start(bf16[32,256]{1,0:T(8,128)(2,1)S(1)} %get-tuple-element.7), channel_id=1, source_target_pairs={{0,2},{2,4},{4,6},{6,8},{8,10},{10,12},{12,14},{14,0},{1,3},{3,5},... | collective-permute-start | bytes 49160 | tf_op jit(solution)/shard_map/ppermute | solution.py:11
  70.7 5.0 %collective-permute-start.7 = (bf16[32,256]{1,0:T(8,128)(2,1)S(1)}, bf16[32,256]{1,0:T(8,128)(2,1)S(1)}, u32[]{:S(2)}, u32[]{:S(2)}) collective-permute-start(bf16[32,256]{1,0:T(8,128)(2,1)S(1)} %get-tuple-element.8), channel_id=1, source_target_pairs={{0,14},{2,0},{4,2},{6,4},{8,6},{10,8},{12,10},{14,12},{1,15},{3,1}... | collective-permute-start | bytes 49160 | tf_op jit(solution)/shard_map/ppermute | solution.py:11
  74.0 3.7 %collective-permute-start.6 = (bf16[32,256]{1,0:T(8,128)(2,1)S(1)}, bf16[32,256]{1,0:T(8,128)(2,1)S(1)}, u32[]{:S(2)}, u32[]{:S(2)}) collective-permute-start(bf16[32,256]{1,0:T(8,128)(2,1)S(1)} %get-tuple-element.5), channel_id=1, source_target_pairs={{0,12},{2,14},{4,0},{6,2},{8,4},{10,6},{12,8},{14,10},{1,13},{3,15... | collective-permute-start | bytes 49160 | tf_op jit(solution)/shard_map/ppermute | solution.py:11
  78.1 2.9 %copy-start.4 = (bf16[512,256]{1,0:T(8,128)(2,1)S(1)}, bf16[512,256]{1,0:T(8,128)(2,1)}, u32[]{:S(2)}) copy-start(bf16[512,256]{1,0:T(8,128)(2,1)} %param.23) | copy-start | bytes 786436
  82.4 91.5 %all-reduce.3.cloned.1.call-start = ((), (), s32[]{:S(2)}) async-start(), calls=%async_computation.6 | async-start | bytes 2097152 | tf_op jit(solution)/shard_map/psum | solution.py:122
  86.9 3.0 %copy-start.3 = (bf16[256,256]{1,0:T(8,128)(2,1)S(1)}, bf16[256,256]{1,0:T(8,128)(2,1)}, u32[]{:S(2)}) copy-start(bf16[256,256]{1,0:T(8,128)(2,1)} %param.13) | copy-start | bytes 393220
  (3 other events, 5.8 us)
Sparse Core Ops, SparseCore 0:
  25.6 7.9 reduce-scatter.3
  57.4 8.6 reduce-scatter.5
  82.5 7.3 reduce-scatter.7
  94.3 79.5 all-reduce.2
where the time goes:
time: 184 us; the launch traced here: 183 us
  waiting for transfers between devices  118 us (64%)
  starting transfers between devices  19.6 us (11%)
  matrix products  14.3 us (8%)
  between operations  14 us (8%)
  blocking collectives  8.75 us (5%)
  local copies, waits for them, and re-layouts  4.5 us (2%)
  other arithmetic  4 us (2%)
    psum x1, waiting for transfers between devices, on_device(): grad_up, grad_down = lax.psum((up_part, down_part), ('mesh', 'grid'))  82.4 us
    reduce_scatter x3, waiting for transfers between devices, mlp_block(): lax.psum_scatter(partial_sum, 'mp', scatter_dimension=1, tiled=True)  19.8 us
    ppermute x8, starting transfers between devices, passed_along(): lax.ppermute(shard, axis, [(i, (i + by) % devices) for i in range(devices)])  14.9 us
    all_gather x4, blocking collectives, widen(): return lax.all_gather(values, 'mp', axis=1, tiled=True)  8.75 us
    ppermute x1, waiting for transfers between devices, with_halo(): after = lax.ppermute(initial, axis, down)  6.04 us
    ppermute x1, waiting for transfers between devices, with_halo(): before = lax.ppermute(last, axis, up)  4.9 us
    ppermute x8, waiting for transfers between devices, passed_along(): lax.ppermute(shard, axis, [(i, (i + by) % devices) for i in range(devices)])  4.78 us
    ppermute x1, starting transfers between devices, with_halo(): after = lax.ppermute(initial, axis, down)  4.52 us
  transfers between devices with their start and end apart: 14, of which 9 were waited for; matrix products, arithmetic and copies ran while one was open for 3% of the time, Pallas kernels for 0%

commit v1 on v0

v1 whole, which is shorter than its diff:
```python
import functools

import jax
import jax.numpy as jnp
from jax import lax
from jax.experimental import pallas as pl
from jax.experimental.pallas import tpu as pltpu
from jax.sharding import PartitionSpec as P

MESH = pl.DeviceIdType.MESH
slot_offsets = (-2, -1, 1, 2)
FIRST = (((0,), (0,)), ((), ()))
SECOND = (((1,), (1,)), ((), ()))
LANES = 128


def mm(a, b, dims=(((1,), (0,)), ((), ()))):
    return lax.dot_general(a, b, dims, preferred_element_type=jnp.float32)


def plan(mesh_axis, grid_axis, width, hidden):
    devices = mesh_axis * grid_axis
    total = 2 * width * hidden // LANES
    pieces = max(1, min(4, total // (16 * devices)))
    piece = total // pieces
    by_grid = piece // grid_axis
    return total, pieces, piece, by_grid, by_grid // mesh_axis


def kernel(
    sizes,
    grid_ref,
    mesh_ref,
    targets_ref,
    gslots_ref,
    mslots_ref,
    links_ref,
    ein_ref,
    eout_ref,
    pin_ref,
    pout_ref,
    din_ref,
    dout_ref,
    cot_ref,
    pred_ref,
    red_ref,
    counts,
    local_t,
    picker_t,
    placer,
    out_slots,
    in_slots,
    back_out,
    back_in,
    acc,
    own,
    other,
    part_out,
    part_in,
    keep,
    state,
    before_halo,
    after_halo,
    final,
    gown,
    gother,
    gpart_out,
    gpart_in,
    cot_other,
    hidden_grad,
    grads,
    stage,
    rx,
    acc_x,
    stage_z,
    rz,
    send_sems,
    recv_sems,
):
    mesh_n, grid_n = sizes
    devices = mesh_n * grid_n
    grid_rows, half = grid_ref.shape
    mesh_rows = mesh_ref.shape[0]
    hidden = ein_ref.shape[1]
    width = ein_ref.shape[0]
    cap = gslots_ref.shape[1] // 4
    total, pieces, piece, by_grid, by_mesh = plan(mesh_n, grid_n, width, hidden)
    mz, mx, mp = (lax.axis_index("mesh"), lax.axis_index("grid"), lax.axis_index("mp"))
    place = mz * grid_n + mx
    peer = {"mp": 1 - mp}

    def at(offset):
        spot = lax.rem(place + (devices + offset), devices)
        return {"mesh": lax.div(spot, grid_n), "grid": lax.rem(spot, grid_n)}

    def along(axis, me, count, step):
        return {axis: lax.rem(me + step, count)}

    started = []

    def send(src, dst, device):
        index = len(started)
        copy = pltpu.make_async_remote_copy(
            src_ref=src,
            dst_ref=dst,
            send_sem=send_sems.at[index],
            recv_sem=recv_sems.at[index],
            device_id=device,
            device_id_type=MESH,
        )
        copy.start()
        started.append(copy)
        return copy

    partners = [peer] + [at(o) for o in slot_offsets]
    partners += [along("grid", mx, grid_n, d) for d in range(1, grid_n)]
    partners += [along("mesh", mz, mesh_n, d) for d in range(1, mesh_n)]
    barrier = pltpu.get_barrier_semaphore()
    for device in partners:
        pl.semaphore_signal(barrier, inc=1, device_id=device, device_id_type=MESH)

    rows_at = lambda n, m: lax.broadcasted_iota(jnp.int32, (n, m), 0)
    picker_t[...] = (
        (rows_at(grid_rows, 4 * cap) == gslots_ref[...]).astype(jnp.float32).astype(jnp.bfloat16)
    )
    placer[...] = (
        (rows_at(mesh_rows, 4 * cap) == mslots_ref[...]).astype(jnp.float32).astype(jnp.bfloat16)
    )
    out_slots[...] = mm(picker_t[...], grid_ref[...], FIRST).astype(jnp.bfloat16)
    pl.semaphore_wait(barrier, len(partners))

    slots = []
    for k, offset in enumerate(slot_offsets):
        rows = pl.ds(k * cap, cap)
        slots.append(send(out_slots.at[rows], in_slots.at[rows], at(offset)))
    cot_copy = send(cot_ref, cot_other, peer)

    def count_into(dst, src_ref, block):
        rows, span = dst.shape
        columns = src_ref.shape[1]

        def body(i, carry):
            here = pl.ds(pl.multiple_of(i * block, block), block)
            window = lax.broadcasted_iota(jnp.int32, (block, span), 1)
            links = src_ref[here, :]
            found = jnp.zeros((block, span), jnp.float32)
            for k in range(columns):
                found = found + (links[:, k : k + 1] == window).astype(jnp.float32)
            dst[here, :] = found.astype(jnp.bfloat16)
            return carry

        lax.fori_loop(0, rows // block, body, 0)

    count_into(local_t, targets_ref, 32)
    chunk = 256
    chunks = mesh_rows // chunk
    chunk_rows = [pl.ds(c * chunk, chunk) for c in range(chunks)]
    for rows in chunk_rows:
        acc[rows, :] = mm(local_t[:, rows], grid_ref[...], FIRST)

    first = pl.ds(pl.multiple_of(mp * half, half), half)
    second = pl.ds(pl.multiple_of((1 - mp) * half, half), half)

    def normalise(mine, theirs):
        a, b = (mine.astype(jnp.float32), theirs.astype(jnp.float32))
        mean = (jnp.sum(a, axis=1, keepdims=True) + jnp.sum(b, axis=1, keepdims=True)) / width
        a, b = (a - mean, b - mean)
        spread = jnp.sum(a * a, axis=1, keepdims=True) + jnp.sum(b * b, axis=1, keepdims=True)
        scale = lax.rsqrt(spread / width + 1e-05)
        return ((a * scale).astype(jnp.bfloat16), (b * scale).astype(jnp.bfloat16))

    def hidden_units(mine, theirs, in_ref):
        na, nb = normalise(mine, theirs)
        return (na, nb, mm(na, in_ref[first, :]) + mm(nb, in_ref[second, :]))

    def widen(which, rows):
        return send(own.at[which, rows], other.at[which, rows], peer)

    def mesh_block(which, wide, in_ref, out_ref, base_ref, dst_ref, after):
        parts = []
        for rows, copy in zip(chunk_rows, wide):
            copy.wait_recv()
            before = hidden_units(own[which, rows, :], other[which, rows, :], in_ref)[2]
            activated = (before * jax.nn.sigmoid(before)).astype(jnp.bfloat16)
            part_out[which, rows, :] = mm(activated, out_ref[:, second]).astype(jnp.bfloat16)
            parts.append(send(part_out.at[which, rows], part_in.at[which, rows], peer))
            keep[rows, :] = mm(activated, out_ref[:, first]) + base_ref[rows, :].astype(jnp.float32)
        for rows, copy in zip(chunk_rows, parts):
            copy.wait_recv()
            dst_ref[rows, :] = (
                keep[rows, :] + part_in[which, rows, :].astype(jnp.float32)
            ).astype(jnp.bfloat16)
            after(rows)

    for copy in slots:
        copy.wait_recv()
    wide = []
    for rows in chunk_rows:
        own[0, rows, :] = (mm(placer[rows, :], in_slots[...]) + acc[rows, :]).astype(jnp.bfloat16)
        wide.append(widen(0, rows))

    count_into(counts, links_ref, 32)
    halo = []

    def send_halo(rows):
        halo.append(send(state.at[rows], before_halo.at[rows], at(1)))
        halo.append(send(state.at[rows], after_halo.at[rows], at(-1)))

    mesh_block(0, wide, ein_ref, eout_ref, mesh_ref, state, send_halo)

    cot_copy.wait_recv()
    hidden_grad[...] = mm(cot_ref[...], dout_ref[:, first], SECOND) + mm(
        cot_other[...], dout_ref[:, second], SECOND
    )
    for rows in chunk_rows:
        acc[rows, :] = mm(counts[rows, mesh_rows : 2 * mesh_rows], state[...])
    for copy in halo:
        copy.wait_recv()
    wide = []
    for rows in chunk_rows:
        own[1, rows, :] = (
            acc[rows, :]
            + mm(counts[rows, :mesh_rows], before_halo[...])
            + mm(counts[rows, 2 * mesh_rows :], after_halo[...])
        ).astype(jnp.bfloat16)
        wide.append(widen(1, rows))
    mesh_block(1, wide, pin_ref, pout_ref, state, final, lambda rows: None)

    back_out[...] = mm(placer[...], final[...], FIRST).astype(jnp.bfloat16)
    slots = []
    for k, offset in enumerate(slot_offsets):
        rows = pl.ds(k * cap, cap)
        slots.append(send(back_out.at[rows], back_in.at[rows], at(-offset)))
    grid_sum = mm(local_t[...], final[...])
    for copy in slots:
        copy.wait_recv()
    gown[...] = (grid_sum + mm(picker_t[...], back_in[...])).astype(jnp.bfloat16)
    send(gown, gother, peer).wait_recv()
    normed_a, normed_b, before = hidden_units(gown[...], gother[...], din_ref)
    gate = jax.nn.sigmoid(before)
    activated = (before * gate).astype(jnp.bfloat16)

    def put(row, values):
        rows = pl.ds(row, values.shape[0])
        grads[rows, :] = values
        stage[rows, :] = values.astype(jnp.bfloat16)

    blocks = half // LANES
    for side, cot in ((mp, cot_ref), (1 - mp, cot_other)):
        down = mm(activated, cot[...], FIRST)
        for b in range(blocks):
            row = pl.multiple_of((side * blocks + b) * hidden, hidden)
            put(row, down[:, b * LANES : (b + 1) * LANES])

    grid_sums = []

    def reduce_grid(i):
        copies = []
        for d in range(1, grid_n):
            to = lax.rem(mx + d, grid_n)
            rows = pl.ds(pl.multiple_of(i * piece + to * by_grid, by_grid), by_grid)
            copies.append(send(stage.at[rows], rx.at[i, d - 1], along("grid", mx, grid_n, d)))
        grid_sums.append(copies)

    ready = pieces // 2
    for i in range(ready):
        reduce_grid(i)

    before_grad = (hidden_grad[...] * gate * (1.0 + before * (1.0 - gate))).astype(jnp.bfloat16)
    for side, normed in ((mp, normed_a), (1 - mp, normed_b)):
        up = mm(normed, before_grad, FIRST)
        for b in range(hidden // LANES):
            row = pl.multiple_of(total // 2 + b * width + side * half, half)
            put(row, up[:, b * LANES : (b + 1) * LANES])
    for i in range(ready, pieces):
        reduce_grid(i)

    gpart_out[...] = mm(activated, dout_ref[:, second]).astype(jnp.bfloat16)
    decoded = send(gpart_out, gpart_in, peer)
    gkeep = mm(activated, dout_ref[:, first]) + grid_ref[...].astype(jnp.float32)

    mesh_sums = []
    for i in range(pieces):
        mine = pl.ds(pl.multiple_of(i * piece + mx * by_grid, by_grid), by_grid)
        value = grads[mine, :]
        for d, copy in enumerate(grid_sums[i]):
            copy.wait_recv()
            value = value + rx[i, d].astype(jnp.float32)
        acc_x[i] = value
        stage_z[i] = value.astype(jnp.bfloat16)
        copies = []
        for d in range(1, mesh_n):
            to = lax.rem(mz + d, mesh_n)
            rows = pl.ds(pl.multiple_of(to * by_mesh, by_mesh), by_mesh)
            copies.append(send(stage_z.at[i, rows], rz.at[i, d - 1], along("mesh", mz, mesh_n, d)))
        mesh_sums.append(copies)

    decoded.wait_recv()
    pred_ref[...] = (gkeep + gpart_in[...].astype(jnp.float32)).astype(jnp.bfloat16)

    spread_mesh = []
    for i in range(pieces):
        value = acc_x[i, pl.ds(pl.multiple_of(mz * by_mesh, by_mesh), by_mesh), :]
        for d, copy in enumerate(mesh_sums[i]):
            copy.wait_recv()
            value = value + rz[i, d].astype(jnp.float32)
        start = i * piece + mx * by_grid + mz * by_mesh
        rows = pl.ds(pl.multiple_of(start, by_mesh), by_mesh)
        red_ref[rows, :] = value.astype(jnp.bfloat16)
        spread_mesh.append(
            [
                send(red_ref.at[rows], red_ref.at[rows], along("mesh", mz, mesh_n, d))
                for d in range(1, mesh_n)
            ]
        )
    spread_grid = []
    for i in range(pieces):
        for copy in spread_mesh[i]:
            copy.wait_recv()
        rows = pl.ds(pl.multiple_of(i * piece + mx * by_grid, by_grid), by_grid)
        spread_grid += [
            send(red_ref.at[rows], red_ref.at[rows], along("grid", mx, grid_n, d))
            for d in range(1, grid_n)
        ]
    for copy in spread_grid:
        copy.wait_recv()
    for copy in started:
        copy.wait_send()


def on_device(sizes, *args):
    mesh_n, grid_n = sizes
    grid_latent, mesh_latent, local_targets, grid_slots, mesh_slots, mesh_links = args[:6]
    weights, cotangent = (args[6:12], args[12])
    grid_rows, half = grid_latent.shape
    mesh_rows = mesh_latent.shape[0]
    width, hidden = weights[0].shape
    cap4 = grid_slots.size
    total, pieces, piece, by_grid, by_mesh = plan(mesh_n, grid_n, width, hidden)
    copies = 4 + 1 + 4 + 4 + 4 + 4 + 1 + 1 + 2 * pieces * (grid_n - 1 + mesh_n - 1)
    bf16, f32 = (jnp.bfloat16, jnp.float32)
    scratch = [
        ((mesh_rows, 3 * mesh_rows), bf16),
        ((grid_rows, mesh_rows), bf16),
        ((grid_rows, cap4), bf16),
        ((mesh_rows, cap4), bf16),
        ((cap4, half), bf16),
        ((cap4, half), bf16),
        ((cap4, half), bf16),
        ((cap4, half), bf16),
        ((mesh_rows, half), f32),
        ((2, mesh_rows, half), bf16),
        ((2, mesh_rows, half), bf16),
        ((2, mesh_rows, half), bf16),
        ((2, mesh_rows, half), bf16),
        ((mesh_rows, half), f32),
        ((mesh_rows, half), bf16),
        ((mesh_rows, half), bf16),
        ((mesh_rows, half), bf16),
        ((mesh_rows, half), bf16),
        ((grid_rows, half), bf16),
        ((grid_rows, half), bf16),
        ((grid_rows, half), bf16),
        ((grid_rows, half), bf16),
        ((grid_rows, half), bf16),
        ((grid_rows, hidden), f32),
        ((total, LANES), f32),
        ((total, LANES), bf16),
        ((pieces, grid_n - 1, by_grid, LANES), bf16),
        ((pieces, by_grid, LANES), f32),
        ((pieces, by_grid, LANES), bf16),
        ((pieces, mesh_n - 1, by_mesh, LANES), bf16),
    ]
    vmem = pl.BlockSpec(memory_space=pltpu.VMEM)
    prediction, reduced = pl.pallas_call(
        functools.partial(kernel, sizes),
        out_shape=(
            jax.ShapeDtypeStruct((grid_rows, half), bf16),
            jax.ShapeDtypeStruct((total, LANES), bf16),
        ),
        in_specs=[vmem] * 13,
        out_specs=(vmem, vmem),
        scratch_shapes=[pltpu.VMEM(shape, dtype) for shape, dtype in scratch]
        + [pltpu.SemaphoreType.DMA((copies,)), pltpu.SemaphoreType.DMA((copies,))],
        compiler_params=pltpu.CompilerParams(
            collective_id=0, has_side_effects=True, vmem_limit_bytes=40 * 1024 * 1024
        ),
        name="forecast",
    )(
        grid_latent,
        mesh_latent,
        local_targets,
        grid_slots.reshape(1, cap4),
        mesh_slots.reshape(1, cap4),
        mesh_links,
        *weights,
        cotangent,
    )
    wide = reduced.astype(f32)
    down = wide[: total // 2].reshape(width // LANES, hidden, LANES)
    up = wide[total // 2 :].reshape(hidden // LANES, width, LANES)
    grad_down = jnp.concatenate([down[b] for b in range(down.shape[0])], axis=1)
    grad_up = jnp.concatenate([up[b] for b in range(up.shape[0])], axis=1)
    return (prediction, grad_up, grad_down)


def solution(mesh):
    sizes = (mesh.shape["mesh"], mesh.shape["grid"])
    rows = P(("groups", "mesh", "grid"), "mp")
    index = P(("mesh", "grid"), None)
    weights = (P(None, "mp"), P("mp", None)) * 3
    return jax.shard_map(
        functools.partial(on_device, sizes),
        mesh=mesh,
        in_specs=(rows, rows, index, index, index, index, *weights, rows),
        out_specs=(rows, P("groups", "mp"), P(("groups", "mp"), None)),
        check_vma=False,
    )
```

time: 184 us -> 71 us (0.39)
  waiting for transfers between devices: 118 us -> 0 us
  Pallas kernels: 0 us -> 58.3 us
  starting transfers between devices: 19.6 us -> 0 us
  matrix products: 14.3 us -> 0 us
  between operations: 14 us -> 0.72 us
  blocking collectives: 8.75 us -> 0 us
  local copies, waits for them, and re-layouts: 4.5 us -> 9.94 us
  other arithmetic: 4 us -> 1.66 us
    psum x1 -> x0, waiting for transfers between devices: 82.4 us -> none  [on_device(): grad_up, grad_down = lax.psum((up_part, down_part), ('mesh', 'grid'))]
    pallas_call x0 -> x1, Pallas kernels: none -> 58.3 us  [on_device(): pl.pallas_call(functools.partial(kernel, sizes), out_shape=(jax.ShapeDtyp...]
    reduce_scatter x3 -> x0, waiting for transfers between devices: 19.8 us -> none  [mlp_block(): lax.psum_scatter(partial_sum, 'mp', scatter_dimension=1, tiled=True)]
    ppermute x10 -> x0, starting transfers between devices: 19.4 us -> none  [the longest x8 14.9 us: passed_along(): lax.ppermute(shard, axis, [(i, (i + by) % devices) for i in range(devices)])]
    ppermute x10 -> x0, waiting for transfers between devices: 15.7 us -> none  [the longest x1 6.04 us: with_halo(): after = lax.ppermute(initial, axis, down)]
    dot_general x13 -> x0, matrix products: 14.3 us -> none  [the longest x3 4.45 us: mlp_block(): jnp.dot(activated, weight_out, preferred_element_type=jnp.float32)]
    all_gather x4 -> x0, blocking collectives: 8.75 us -> none  [widen(): return lax.all_gather(values, 'mp', axis=1, tiled=True)]
    unnamed x28 -> x23, local copies, waits for them, and re-layouts: 2.79 us -> 8.3 us
  transfers between devices with their start and end apart: 14 -> 0, of which waited for: 9 -> 0; matrix products, arithmetic and copies ran while one was open for 3% -> 0% of each run, Pallas kernels for 0% -> 0%
where the time goes in v1:
time: 71 us; the launch traced here: 70.6 us
  Pallas kernels  58.3 us (82%)
  local copies, waits for them, and re-layouts  9.94 us (14%)
  other arithmetic  1.66 us (2%)
  between operations  0.72 us (1%)
    pallas_call x1, Pallas kernels, on_device(): pl.pallas_call(functools.partial(kernel, sizes), out_shape=(jax.ShapeDtyp...  58.3 us
    unnamed x23, local copies, waits for them, and re-layouts  8.3 us

profile of v1, /device:TPU:0, one launch (start us, length us, event | category | flops | bytes accessed | tf_op | source)
XLA Modules:
  0.0 70.6 jit_solution(6906388357668179335)
XLA Ops:
  0.6 0.0 copy-start.9
  0.6 0.0 copy-start
  0.7 0.8 %reshape.26.gslots_ref = s32[1,128]{1,0:T(1,128)S(1)} reshape(s32[4,32]{1,0:T(4,128)} %param.16) | data formatting | bytes 1024 | tf_op jit(solution)/shard_map/reshape | solution.py:393
  1.5 0.8 %reshape.27.mslots_ref = s32[1,128]{1,0:T(1,128)S(1)} reshape(s32[4,32]{1,0:T(4,128)} %param.17) | data formatting | bytes 1024 | tf_op jit(solution)/shard_map/reshape | solution.py:394
  2.2 0.0 copy-done.9
  2.2 0.1 copy.16.targets_ref
  2.4 0.0 copy-start.7
  2.4 0.9 %copy.17.links_ref = s32[512,6]{1,0:T(8,128)S(1)} copy(s32[512,6]{0,1:T(8,128)} %param.18) | data formatting | bytes 24576 | tf_op args[5]
  3.3 0.0 copy-done
  3.3 0.0 copy-done.7
  3.3 0.0 copy-start.1
  3.3 0.9 %copy-done.1 = bf16[512,256]{1,0:T(8,128)(2,1)S(1)} copy-done((bf16[512,256]{1,0:T(8,128)(2,1)S(1)}, bf16[512,256]{1,0:T(8,128)(2,1)}, u32[]{:S(2)}) %copy-start.1) | copy-done | bytes 262168
  4.3 0.0 copy-start.2
  4.3 0.9 %copy-done.2 = bf16[256,512]{1,0:T(8,128)(2,1)S(1)} copy-done((bf16[256,512]{1,0:T(8,128)(2,1)S(1)}, bf16[256,512]{1,0:T(8,128)(2,1)}, u32[]{:S(2)}) %copy-start.2) | copy-done | bytes 262168
  5.2 0.0 copy-start.3
  5.2 0.9 %copy-done.3 = bf16[512,256]{1,0:T(8,128)(2,1)S(1)} copy-done((bf16[512,256]{1,0:T(8,128)(2,1)S(1)}, bf16[512,256]{1,0:T(8,128)(2,1)}, u32[]{:S(2)}) %copy-start.3) | copy-done | bytes 262168
  6.2 0.9 %copy-done.4 = bf16[256,512]{1,0:T(8,128)(2,1)S(1)} copy-done((bf16[256,512]{1,0:T(8,128)(2,1)S(1)}, bf16[256,512]{1,0:T(8,128)(2,1)}, u32[]{:S(2)}) %copy-start.4) | copy-done | bytes 262168
  7.1 0.9 %copy-done.5 = bf16[512,256]{1,0:T(8,128)(2,1)S(1)} copy-done((bf16[512,256]{1,0:T(8,128)(2,1)S(1)}, bf16[512,256]{1,0:T(8,128)(2,1)}, u32[]{:S(2)}) %copy-start.5) | copy-done | bytes 262168
  8.1 0.9 %copy-done.6 = bf16[256,512]{1,0:T(8,128)(2,1)S(1)} copy-done((bf16[256,512]{1,0:T(8,128)(2,1)S(1)}, bf16[256,512]{1,0:T(8,128)(2,1)}, u32[]{:S(2)}) %copy-start.6) | copy-done | bytes 262168
  9.0 0.9 %copy-done.8 = bf16[256,256]{1,0:T(8,128)(2,1)S(1)} copy-done((bf16[256,256]{1,0:T(8,128)(2,1)S(1)}, bf16[256,256]{1,0:T(8,128)(2,1)}, u32[]{:S(2)}) %copy-start.8) | copy-done | bytes 131096
  9.9 58.3 %forecast.1 = (bf16[256,256]{1,0:T(8,128)(2,1)S(1)}, bf16[2048,128]{1,0:T(8,128)(2,1)S(1)}) custom-call(bf16[256,256]{1,0:T(8,128)(2,1)S(1)} %copy-done.7, bf16[512,256]{1,0:T(8,128)(2,1)S(1)} %copy-done, s32[256,3]{1,0:T(8,128)S(1)} %copy.16.targets_ref, s32[1,128]{1,0:T(1,128)S(1)} %reshape.26.gslots_ref, s32[1,128]{1,0:T(1,128)S(1)} %reshape.27.mslots_ref, ...), custom_call_target="tpu_custom_call" | custom-call | tf_op jit(solution)/shard_map/forecast/pallas_call | solution.py:375
  68.3 0.8 %pad_maximum_fusion.1 = f32[256,512]{1,0:T(8,128)} fusion(f32[256,128]{1,0:T(8,128)S(1)} %get-tuple-element.10, f32[256,128]{1,0:T(8,128)S(1)} %get-tuple-element.9, f32[256,128]{1,0:T(8,128)S(1)} %get-tuple-element.8, f32[256,128]{1,0:T(8,128)S(1)} %get-tuple-element.7), kind=kLoop, calls=%fused_computation.1 | loop fusion | flops 393216 | bytes 1048576 | tf_op jit(solution)/shard_map/concatenate | solution.py:402
  69.1 0.8 %pad_maximum_fusion = f32[512,256]{1,0:T(8,128)} fusion(f32[512,128]{1,0:T(8,128)S(1)} %get-tuple-element.12, f32[512,128]{1,0:T(8,128)S(1)} %get-tuple-element.11), kind=kLoop, calls=%fused_computation | loop fusion | flops 131072 | bytes 1048576 | tf_op jit(solution)/shard_map/concatenate | solution.py:403
  70.0 0.7 copy.19
  (6 shorter events, 0.1 us)
Async XLA Ops:
  0.6 1.6 %copy-start.9 = (s32[256,3]{0,1:T(4,128)S(1)}, s32[256,3]{0,1:T(4,128)}, u32[]{:S(2)}) copy-start(s32[256,3]{0,1:T(4,128)} %param.15) | copy-start | bytes 9220
  0.6 2.6 %copy-start = (bf16[512,256]{1,0:T(8,128)(2,1)S(1)}, bf16[512,256]{1,0:T(8,128)(2,1)}, u32[]{:S(2)}) copy-start(bf16[512,256]{1,0:T(8,128)(2,1)} %mesh_ref.1) | copy-start | bytes 786436
  2.4 0.9 %copy-start.7 = (bf16[256,256]{1,0:T(8,128)(2,1)S(1)}, bf16[256,256]{1,0:T(8,128)(2,1)}, u32[]{:S(2)}) copy-start(bf16[256,256]{1,0:T(8,128)(2,1)} %grid_ref.1) | copy-start | bytes 393220
  3.3 1.0 %copy-start.1 = (bf16[512,256]{1,0:T(8,128)(2,1)S(1)}, bf16[512,256]{1,0:T(8,128)(2,1)}, u32[]{:S(2)}) copy-start(bf16[512,256]{1,0:T(8,128)(2,1)} %ein_ref.1) | copy-start | bytes 786436
  4.3 0.9 %copy-start.2 = (bf16[256,512]{1,0:T(8,128)(2,1)S(1)}, bf16[256,512]{1,0:T(8,128)(2,1)}, u32[]{:S(2)}) copy-start(bf16[256,512]{1,0:T(8,128)(2,1)} %eout_ref.1) | copy-start | bytes 786436
  5.2 0.9 %copy-start.3 = (bf16[512,256]{1,0:T(8,128)(2,1)S(1)}, bf16[512,256]{1,0:T(8,128)(2,1)}, u32[]{:S(2)}) copy-start(bf16[512,256]{1,0:T(8,128)(2,1)} %pin_ref.1) | copy-start | bytes 786436
  6.2 0.9 %copy-start.4 = (bf16[256,512]{1,0:T(8,128)(2,1)S(1)}, bf16[256,512]{1,0:T(8,128)(2,1)}, u32[]{:S(2)}) copy-start(bf16[256,512]{1,0:T(8,128)(2,1)} %pout_ref.1) | copy-start | bytes 786436
  7.1 0.9 %copy-start.5 = (bf16[512,256]{1,0:T(8,128)(2,1)S(1)}, bf16[512,256]{1,0:T(8,128)(2,1)}, u32[]{:S(2)}) copy-start(bf16[512,256]{1,0:T(8,128)(2,1)} %din_ref.1) | copy-start | bytes 786436
  8.1 0.9 %copy-start.6 = (bf16[256,512]{1,0:T(8,128)(2,1)S(1)}, bf16[256,512]{1,0:T(8,128)(2,1)}, u32[]{:S(2)}) copy-start(bf16[256,512]{1,0:T(8,128)(2,1)} %dout_ref.1) | copy-start | bytes 786436
  9.0 0.9 %copy-start.8 = (bf16[256,256]{1,0:T(8,128)(2,1)S(1)}, bf16[256,256]{1,0:T(8,128)(2,1)}, u32[]{:S(2)}) copy-start(bf16[256,256]{1,0:T(8,128)(2,1)} %cot_ref.1) | copy-start | bytes 393220

commit v2 on v1

--- a/solution.py
+++ b/solution.py
@@ -29,6 +29,21 @@
 
 def kernel(
     sizes,
+    grid_hbm,
+    mesh_hbm,
+    targets_hbm,
+    gslots_hbm,
+    mslots_hbm,
+    links_hbm,
+    ein_hbm,
+    eout_hbm,
+    pin_hbm,
+    pout_hbm,
+    din_hbm,
+    dout_hbm,
+    cot_hbm,
+    pred_ref,
+    red_ref,
     grid_ref,
     mesh_ref,
     targets_ref,
@@ -42,8 +57,9 @@
     din_ref,
     dout_ref,
     cot_ref,
-    pred_ref,
-    red_ref,
+    links_col,
+    targets_col,
+    placer_rows,
     counts,
     local_t,
     picker_t,
@@ -59,8 +75,7 @@
     part_in,
     keep,
     state,
-    before_halo,
-    after_halo,
+    halo,
     final,
     gown,
     gother,
@@ -76,6 +91,7 @@
     rz,
     send_sems,
     recv_sems,
+    load_sems,
 ):
     mesh_n, grid_n = sizes
     devices = mesh_n * grid_n
@@ -83,8 +99,31 @@
     mesh_rows = mesh_ref.shape[0]
     hidden = ein_ref.shape[1]
     width = ein_ref.shape[0]
-    cap = gslots_ref.shape[1] // 4
+    cap = gslots_ref.shape[1]
     total, pieces, piece, by_grid, by_mesh = plan(mesh_n, grid_n, width, hidden)
+    loads = {}
+    for name, src, dst in (
+        ("grid", grid_hbm, grid_ref),
+        ("gslots", gslots_hbm, gslots_ref),
+        ("targets", targets_hbm, targets_ref),
+        ("mslots", mslots_hbm, mslots_ref),
+        ("cot", cot_hbm, cot_ref),
+        ("ein", ein_hbm, ein_ref),
+        ("eout", eout_hbm, eout_ref),
+        ("mesh", mesh_hbm, mesh_ref),
+        ("links", links_hbm, links_ref),
+        ("dout", dout_hbm, dout_ref),
+        ("pin", pin_hbm, pin_ref),
+        ("pout", pout_hbm, pout_ref),
+        ("din", din_hbm, din_ref),
+    ):
+        loads[name] = pltpu.make_async_copy(src, dst, load_sems.at[len(loads)])
+        loads[name].start()
+
+    def loaded(*wanted):
+        for name in wanted:
+            loads[name].wait()
+
     mz, mx, mp = (lax.axis_index("mesh"), lax.axis_index("grid"), lax.axis_index("mp"))
     place = mz * grid_n + mx
     peer = {"mp": 1 - mp}
@@ -120,12 +159,12 @@
         pl.semaphore_signal(barrier, inc=1, device_id=device, device_id_type=MESH)
 
     rows_at = lambda n, m: lax.broadcasted_iota(jnp.int32, (n, m), 0)
+    row_of = lambda ref: jnp.concatenate([ref[k : k + 1, :] for k in range(4)], axis=1)
+    loaded("gslots")
     picker_t[...] = (
-        (rows_at(grid_rows, 4 * cap) == gslots_ref[...]).astype(jnp.float32).astype(jnp.bfloat16)
+        (rows_at(grid_rows, 4 * cap) == row_of(gslots_ref)).astype(jnp.float32).astype(jnp.bfloat16)
     )
-    placer[...] = (
-        (rows_at(mesh_rows, 4 * cap) == mslots_ref[...]).astype(jnp.float32).astype(jnp.bfloat16)
-    )
+    loaded("grid")
     out_slots[...] = mm(picker_t[...], grid_ref[...], FIRST).astype(jnp.bfloat16)
     pl.semaphore_wait(barrier, len(partners))
 
@@ -133,14 +172,23 @@
     for k, offset in enumerate(slot_offsets):
         rows = pl.ds(k * cap, cap)
         slots.append(send(out_slots.at[rows], in_slots.at[rows], at(offset)))
+    loaded("cot")
     cot_copy = send(cot_ref, cot_other, peer)
-
-    def count_into(dst, src_ref, block):
-        rows, span = dst.shape
-        columns = src_ref.shape[1]
+    loaded("mslots")
+    placed = (rows_at(mesh_rows, 4 * cap) == row_of(mslots_ref)).astype(jnp.float32)
+    placer[...] = placed.astype(jnp.bfloat16)
+
+    def stand_up(ref):
+        table = ref[...]
+        missing = 8 - table.shape[0]
+        table = jnp.concatenate([table, jnp.zeros((missing, table.shape[1]), jnp.int32)], axis=0)
+        return jnp.transpose(table)
+
+    def count_into(dst, src_ref, columns, start, rows, block):
+        span = dst.shape[1]
 
         def body(i, carry):
-            here = pl.ds(pl.multiple_of(i * block, block), block)
+            here = pl.ds(pl.multiple_of(start + i * block, block), block)
             window = lax.broadcasted_iota(jnp.int32, (block, span), 1)
             links = src_ref[here, :]
             found = jnp.zeros((block, span), jnp.float32)
@@ -151,7 +199,9 @@
 
         lax.fori_loop(0, rows // block, body, 0)
 
-    count_into(local_t, targets_ref, 32)
+    loaded("targets")
+    targets_col[...] = stand_up(targets_ref)
+    count_into(local_t, targets_col, targets_ref.shape[0], 0, grid_rows, 32)
     chunk = 256
     chunks = mesh_rows // chunk
     chunk_rows = [pl.ds(c * chunk, chunk) for c in range(chunks)]
@@ -199,34 +249,68 @@
         own[0, rows, :] = (mm(placer[rows, :], in_slots[...]) + acc[rows, :]).astype(jnp.bfloat16)
         wide.append(widen(0, rows))
 
-    count_into(counts, links_ref, 32)
-    halo = []
+    hop = 128
+    arriving = []
 
     def send_halo(rows):
-        halo.append(send(state.at[rows], before_halo.at[rows], at(1)))
-        halo.append(send(state.at[rows], after_halo.at[rows], at(-1)))
-
+        for k in range(rows.size // hop):
+            part = pl.ds(rows.start + k * hop, hop)
+            if grid_n == 2:
+                arriving.append(send(state.at[part], halo.at[mx, part], along("grid", mx, 2, 1)))
+            else:
+                arriving.append(send(state.at[part], halo.at[0, part], at(1)))
+                arriving.append(send(state.at[part], halo.at[1, part], at(-1)))
+
+    loaded("ein", "eout", "mesh")
     mesh_block(0, wide, ein_ref, eout_ref, mesh_ref, state, send_halo)
 
+    loaded("links")
+    links_col[...] = stand_up(links_ref)
+    columns = links_ref.shape[0]
+    steps = mesh_rows // hop
+
+    def side_of(which):
+        return pl.ds(pl.multiple_of(which * (2 * mesh_rows), mesh_rows), mesh_rows)
+
+    def add_side(which):
+        for rows in chunk_rows:
+            acc[rows, :] = acc[rows, :] + mm(counts[rows, side_of(which)], halo[which])
+
+    onward = []
+    for k in range(steps):
+        count_into(counts, links_col, columns, k * hop, hop, 32)
+        if grid_n == 2:
+            part = pl.ds(k * hop, hop)
+            arriving[k].wait_recv()
+            onward.append(send(halo.at[1 - mx, part], halo.at[mx, part], at(2 - 4 * mx)))
+    for rows in chunk_rows:
+        acc[rows, :] = mm(counts[rows, mesh_rows : 2 * mesh_rows], state[...])
+    if grid_n == 2:
+        add_side(1 - mx)
     cot_copy.wait_recv()
+    loaded("dout")
     hidden_grad[...] = mm(cot_ref[...], dout_ref[:, first], SECOND) + mm(
         cot_other[...], dout_ref[:, second], SECOND
     )
-    for rows in chunk_rows:
-        acc[rows, :] = mm(counts[rows, mesh_rows : 2 * mesh_rows], state[...])
-    for copy in halo:
-        copy.wait_recv()
+    placer_rows[...] = jnp.transpose(placed).astype(jnp.bfloat16)
+    if grid_n == 2:
+        for copy in onward:
+            copy.wait_recv()
+        last = (mx,)
+    else:
+        for copy in arriving:
+            copy.wait_recv()
+        last = (0, 1)
     wide = []
     for rows in chunk_rows:
         own[1, rows, :] = (
-            acc[rows, :]
-            + mm(counts[rows, :mesh_rows], before_halo[...])
-            + mm(counts[rows, 2 * mesh_rows :], after_halo[...])
+            acc[rows, :] + sum(mm(counts[rows, side_of(which)], halo[which]) for which in last)
         ).astype(jnp.bfloat16)
         wide.append(widen(1, rows))
+    loaded("pin", "pout", "din")
     mesh_block(1, wide, pin_ref, pout_ref, state, final, lambda rows: None)
 
-    back_out[...] = mm(placer[...], final[...], FIRST).astype(jnp.bfloat16)
+    back_out[...] = mm(placer_rows[...], final[...]).astype(jnp.bfloat16)
     slots = []
     for k, offset in enumerate(slot_offsets):
         rows = pl.ds(k * cap, cap)
@@ -337,9 +421,22 @@
     width, hidden = weights[0].shape
     cap4 = grid_slots.size
     total, pieces, piece, by_grid, by_mesh = plan(mesh_n, grid_n, width, hidden)
-    copies = 4 + 1 + 4 + 4 + 4 + 4 + 1 + 1 + 2 * pieces * (grid_n - 1 + mesh_n - 1)
+    copies = 4 + 1 + 4 + 4 + 4 * mesh_rows // 128 + 4 + 1 + 1 + 2 * pieces * (grid_n - 1 + mesh_n - 1)
     bf16, f32 = (jnp.bfloat16, jnp.float32)
-    scratch = [
+    operands = (
+        grid_latent,
+        mesh_latent,
+        local_targets.T,
+        grid_slots,
+        mesh_slots,
+        mesh_links.T,
+        *weights,
+        cotangent,
+    )
+    scratch = [(x.shape, x.dtype) for x in operands] + [
+        ((mesh_rows, 8), jnp.int32),
+        ((grid_rows, 8), jnp.int32),
+        ((cap4, mesh_rows), bf16),
         ((mesh_rows, 3 * mesh_rows), bf16),
         ((grid_rows, mesh_rows), bf16),
         ((grid_rows, cap4), bf16),
@@ -355,8 +452,7 @@
         ((2, mesh_rows, half), bf16),
         ((mesh_rows, half), f32),
         ((mesh_rows, half), bf16),
-        ((mesh_rows, half), bf16),
-        ((mesh_rows, half), bf16),
+        ((2, mesh_rows, half), bf16),
         ((mesh_rows, half), bf16),
         ((grid_rows, half), bf16),
         ((grid_rows, half), bf16),
@@ -378,24 +474,15 @@
             jax.ShapeDtypeStruct((grid_rows, half), bf16),
             jax.ShapeDtypeStruct((total, LANES), bf16),
         ),
-        in_specs=[vmem] * 13,
+        in_specs=[pl.BlockSpec(memory_space=pltpu.HBM)] * len(operands),
         out_specs=(vmem, vmem),
         scratch_shapes=[pltpu.VMEM(shape, dtype) for shape, dtype in scratch]
-        + [pltpu.SemaphoreType.DMA((copies,)), pltpu.SemaphoreType.DMA((copies,))],
+        + [pltpu.SemaphoreType.DMA((n,)) for n in (copies, copies, len(operands))],
         compiler_params=pltpu.CompilerParams(
             collective_id=0, has_side_effects=True, vmem_limit_bytes=40 * 1024 * 1024
         ),
         name="forecast",
-    )(
-        grid_latent,
-        mesh_latent,
-        local_targets,
-        grid_slots.reshape(1, cap4),
-        mesh_slots.reshape(1, cap4),
-        mesh_links,
-        *weights,
-        cotangent,
-    )
+    )(*operands)
     wide = reduced.astype(f32)
     down = wide[: total // 2].reshape(width // LANES, hidden, LANES)
     up = wide[total // 2 :].reshape(hidden // LANES, width, LANES)

time: 71 us -> 71.1 us (level)
  Pallas kernels: 58.3 us -> 56.3 us
  local copies, waits for them, and re-layouts: 9.94 us -> 11.9 us
    unnamed x23 -> x27, local copies, waits for them, and re-layouts: 8.3 us -> 11.9 us
    pallas_call x1, Pallas kernels: 58.3 us -> 56.3 us  [on_device(): pl.pallas_call(functools.partial(kernel, sizes), out_shape=(jax.ShapeDtyp...]
    reshape x2 -> x0, local copies, waits for them, and re-layouts: 1.57 us -> none  [the longest x1 0.81 us: on_device(): grid_slots.reshape(1, cap4)]
where the time goes in v2:
time: 71.1 us; the launch traced here: 70.5 us
  Pallas kernels  56.3 us (79%)
  local copies, waits for them, and re-layouts  11.9 us (17%)
  other arithmetic  1.66 us (2%)
    pallas_call x1, Pallas kernels, on_device(): pl.pallas_call(functools.partial(kernel, sizes), out_shape=(jax.ShapeDtyp...  56.3 us
    unnamed x27, local copies, waits for them, and re-layouts  11.9 us

profile of v2, /device:TPU:0, one launch (start us, length us, event | category | flops | bytes accessed | tf_op | source)
XLA Modules:
  0.0 70.5 jit_solution(13911575807803187372)
XLA Ops:
  0.6 0.0 copy-start.11
  0.6 0.7 copy-done.11
  1.3 0.0 copy-start
  1.3 0.9 %copy-done = bf16[512,256]{1,0:T(8,128)(2,1)S(1)} copy-done((bf16[512,256]{1,0:T(8,128)(2,1)S(1)}, bf16[512,256]{1,0:T(8,128)(2,1)}, u32[]{:S(2)}) %copy-start) | copy-done | bytes 262168
  2.3 0.0 copy-start.1
  2.3 0.9 %copy-done.1 = bf16[512,256]{1,0:T(8,128)(2,1)S(1)} copy-done((bf16[512,256]{1,0:T(8,128)(2,1)S(1)}, bf16[512,256]{1,0:T(8,128)(2,1)}, u32[]{:S(2)}) %copy-start.1) | copy-done | bytes 262168
  3.2 0.9 %copy-done.2 = bf16[256,512]{1,0:T(8,128)(2,1)S(1)} copy-done((bf16[256,512]{1,0:T(8,128)(2,1)S(1)}, bf16[256,512]{1,0:T(8,128)(2,1)}, u32[]{:S(2)}) %copy-start.2) | copy-done | bytes 262168
  4.2 0.0 copy-start.3
  4.2 0.9 %copy-done.3 = bf16[512,256]{1,0:T(8,128)(2,1)S(1)} copy-done((bf16[512,256]{1,0:T(8,128)(2,1)S(1)}, bf16[512,256]{1,0:T(8,128)(2,1)}, u32[]{:S(2)}) %copy-start.3) | copy-done | bytes 262168
  5.1 0.0 copy-start.4
  5.1 0.9 %copy-done.4 = bf16[256,512]{1,0:T(8,128)(2,1)S(1)} copy-done((bf16[256,512]{1,0:T(8,128)(2,1)S(1)}, bf16[256,512]{1,0:T(8,128)(2,1)}, u32[]{:S(2)}) %copy-start.4) | copy-done | bytes 262168
  6.1 0.0 copy-start.5
  6.1 0.9 %copy-done.5 = bf16[512,256]{1,0:T(8,128)(2,1)S(1)} copy-done((bf16[512,256]{1,0:T(8,128)(2,1)S(1)}, bf16[512,256]{1,0:T(8,128)(2,1)}, u32[]{:S(2)}) %copy-start.5) | copy-done | bytes 262168
  7.0 0.0 copy-start.6
  7.0 0.9 %copy-done.6 = bf16[256,512]{1,0:T(8,128)(2,1)S(1)} copy-done((bf16[256,512]{1,0:T(8,128)(2,1)S(1)}, bf16[256,512]{1,0:T(8,128)(2,1)}, u32[]{:S(2)}) %copy-start.6) | copy-done | bytes 262168
  8.0 0.9 %copy-done.7 = bf16[256,256]{1,0:T(8,128)(2,1)S(1)} copy-done((bf16[256,256]{1,0:T(8,128)(2,1)S(1)}, bf16[256,256]{1,0:T(8,128)(2,1)}, u32[]{:S(2)}) %copy-start.7) | copy-done | bytes 131096
  8.9 0.9 %copy-done.8 = bf16[256,256]{1,0:T(8,128)(2,1)S(1)} copy-done((bf16[256,256]{1,0:T(8,128)(2,1)S(1)}, bf16[256,256]{1,0:T(8,128)(2,1)}, u32[]{:S(2)}) %copy-start.8) | copy-done | bytes 131096
  9.8 0.7 %copy-done.9 = s32[512,6]{0,1:T(8,128)S(1)} copy-done((s32[512,6]{0,1:T(8,128)S(1)}, s32[512,6]{0,1:T(8,128)}, u32[]{:S(2)}) %copy-start.9) | copy-done | bytes 12312
  10.5 0.7 copy-done.10
  11.2 0.7 copy-done.12
  11.9 56.3 %forecast.1 = (bf16[256,256]{1,0:T(8,128)(2,1)S(1)}, bf16[2048,128]{1,0:T(8,128)(2,1)S(1)}) custom-call(bf16[256,256]{1,0:T(8,128)(2,1)S(1)} %copy-done.7, bf16[512,256]{1,0:T(8,128)(2,1)S(1)} %copy-done, s32[3,256]{1,0:T(4,128)S(1)} %bitcast.3, s32[4,32]{1,0:T(4,128)S(1)} %copy-done.11, s32[4,32]{1,0:T(4,128)S(1)} %copy-done.12, s32[6,512]{1,0:T(8,128)S(1)} %bitcast.2, ...), custom_call_target="tpu_custom_call" | custom-call | tf_op jit(solution)/shard_map/forecast/pallas_call | solution.py:471
  68.2 0.8 %pad_maximum_fusion.1 = f32[256,512]{1,0:T(8,128)} fusion(f32[256,128]{1,0:T(8,128)S(1)} %get-tuple-element.10, f32[256,128]{1,0:T(8,128)S(1)} %get-tuple-element.9, f32[256,128]{1,0:T(8,128)S(1)} %get-tuple-element.8, f32[256,128]{1,0:T(8,128)S(1)} %get-tuple-element.7), kind=kLoop, calls=%fused_computation.1 | loop fusion | flops 393216 | bytes 1048576 | tf_op jit(solution)/shard_map/concatenate | solution.py:489
  69.1 0.8 %pad_maximum_fusion = f32[512,256]{1,0:T(8,128)} fusion(f32[512,128]{1,0:T(8,128)S(1)} %get-tuple-element.12, f32[512,128]{1,0:T(8,128)S(1)} %get-tuple-element.11), kind=kLoop, calls=%fused_computation | loop fusion | flops 131072 | bytes 1048576 | tf_op jit(solution)/shard_map/concatenate | solution.py:490
  69.9 0.7 copy.17
  (8 shorter events, 0.1 us)
Async XLA Ops:
  0.6 0.7 copy-start.11
  1.3 0.9 %copy-start = (bf16[512,256]{1,0:T(8,128)(2,1)S(1)}, bf16[512,256]{1,0:T(8,128)(2,1)}, u32[]{:S(2)}) copy-start(bf16[512,256]{1,0:T(8,128)(2,1)} %mesh_hbm.1) | copy-start | bytes 786436
  2.3 0.9 %copy-start.1 = (bf16[512,256]{1,0:T(8,128)(2,1)S(1)}, bf16[512,256]{1,0:T(8,128)(2,1)}, u32[]{:S(2)}) copy-start(bf16[512,256]{1,0:T(8,128)(2,1)} %ein_hbm.1) | copy-start | bytes 786436
  3.2 0.9 %copy-start.2 = (bf16[256,512]{1,0:T(8,128)(2,1)S(1)}, bf16[256,512]{1,0:T(8,128)(2,1)}, u32[]{:S(2)}) copy-start(bf16[256,512]{1,0:T(8,128)(2,1)} %eout_hbm.1) | copy-start | bytes 786436
  4.2 0.9 %copy-start.3 = (bf16[512,256]{1,0:T(8,128)(2,1)S(1)}, bf16[512,256]{1,0:T(8,128)(2,1)}, u32[]{:S(2)}) copy-start(bf16[512,256]{1,0:T(8,128)(2,1)} %pin_hbm.1) | copy-start | bytes 786436
  5.1 0.9 %copy-start.4 = (bf16[256,512]{1,0:T(8,128)(2,1)S(1)}, bf16[256,512]{1,0:T(8,128)(2,1)}, u32[]{:S(2)}) copy-start(bf16[256,512]{1,0:T(8,128)(2,1)} %pout_hbm.1) | copy-start | bytes 786436
  6.1 0.9 %copy-start.5 = (bf16[512,256]{1,0:T(8,128)(2,1)S(1)}, bf16[512,256]{1,0:T(8,128)(2,1)}, u32[]{:S(2)}) copy-start(bf16[512,256]{1,0:T(8,128)(2,1)} %din_hbm.1) | copy-start | bytes 786436
  7.0 0.9 %copy-start.6 = (bf16[256,512]{1,0:T(8,128)(2,1)S(1)}, bf16[256,512]{1,0:T(8,128)(2,1)}, u32[]{:S(2)}) copy-start(bf16[256,512]{1,0:T(8,128)(2,1)} %dout_hbm.1) | copy-start | bytes 786436
  8.0 0.9 %copy-start.7 = (bf16[256,256]{1,0:T(8,128)(2,1)S(1)}, bf16[256,256]{1,0:T(8,128)(2,1)}, u32[]{:S(2)}) copy-start(bf16[256,256]{1,0:T(8,128)(2,1)} %grid_hbm.1) | copy-start | bytes 393220
  8.9 0.9 %copy-start.8 = (bf16[256,256]{1,0:T(8,128)(2,1)S(1)}, bf16[256,256]{1,0:T(8,128)(2,1)}, u32[]{:S(2)}) copy-start(bf16[256,256]{1,0:T(8,128)(2,1)} %cot_hbm.1) | copy-start | bytes 393220
  9.8 0.7 %copy-start.9 = (s32[512,6]{0,1:T(8,128)S(1)}, s32[512,6]{0,1:T(8,128)}, u32[]{:S(2)}) copy-start(s32[512,6]{0,1:T(8,128)} %param.18) | copy-start | bytes 36868
  10.5 0.7 copy-start.10
  11.2 0.7 copy-start.12

commit v3 on v2

--- a/solution.py
+++ b/solution.py
@@ -103,15 +103,15 @@
     total, pieces, piece, by_grid, by_mesh = plan(mesh_n, grid_n, width, hidden)
     loads = {}
     for name, src, dst in (
+        ("gslots", gslots_hbm, gslots_ref),
         ("grid", grid_hbm, grid_ref),
-        ("gslots", gslots_hbm, gslots_ref),
         ("targets", targets_hbm, targets_ref),
+        ("links", links_hbm, links_ref),
         ("mslots", mslots_hbm, mslots_ref),
         ("cot", cot_hbm, cot_ref),
         ("ein", ein_hbm, ein_ref),
         ("eout", eout_hbm, eout_ref),
         ("mesh", mesh_hbm, mesh_ref),
-        ("links", links_hbm, links_ref),
         ("dout", dout_hbm, dout_ref),
         ("pin", pin_hbm, pin_ref),
         ("pout", pout_hbm, pout_ref),
@@ -166,6 +166,27 @@
     )
     loaded("grid")
     out_slots[...] = mm(picker_t[...], grid_ref[...], FIRST).astype(jnp.bfloat16)
+    def stand_up(ref):
+        table = ref[...]
+        missing = 8 - table.shape[0]
+        table = jnp.concatenate([table, jnp.zeros((missing, table.shape[1]), jnp.int32)], axis=0)
+        return jnp.transpose(table)
+
+    def count_into(dst, src_ref, columns, start, rows, block):
+        span = dst.shape[1]
+
+        def body(i, carry):
+            here = pl.ds(pl.multiple_of(start + i * block, block), block)
+            window = lax.broadcasted_iota(jnp.int32, (block, span), 1)
+            links = src_ref[here, :]
+            found = jnp.zeros((block, span), jnp.float32)
+            for k in range(columns):
+                found = found + (links[:, k : k + 1] == window).astype(jnp.float32)
+            dst[here, :] = found.astype(jnp.bfloat16)
+            return carry
+
+        lax.fori_loop(0, rows // block, body, 0)
+
     pl.semaphore_wait(barrier, len(partners))
 
     slots = []
@@ -177,28 +198,6 @@
     loaded("mslots")
     placed = (rows_at(mesh_rows, 4 * cap) == row_of(mslots_ref)).astype(jnp.float32)
     placer[...] = placed.astype(jnp.bfloat16)
-
-    def stand_up(ref):
-        table = ref[...]
-        missing = 8 - table.shape[0]
-        table = jnp.concatenate([table, jnp.zeros((missing, table.shape[1]), jnp.int32)], axis=0)
-        return jnp.transpose(table)
-
-    def count_into(dst, src_ref, columns, start, rows, block):
-        span = dst.shape[1]
-
-        def body(i, carry):
-            here = pl.ds(pl.multiple_of(start + i * block, block), block)
-            window = lax.broadcasted_iota(jnp.int32, (block, span), 1)
-            links = src_ref[here, :]
-            found = jnp.zeros((block, span), jnp.float32)
-            for k in range(columns):
-                found = found + (links[:, k : k + 1] == window).astype(jnp.float32)
-            dst[here, :] = found.astype(jnp.bfloat16)
-            return carry
-
-        lax.fori_loop(0, rows // block, body, 0)
-
     loaded("targets")
     targets_col[...] = stand_up(targets_ref)
     count_into(local_t, targets_col, targets_ref.shape[0], 0, grid_rows, 32)
@@ -208,6 +207,11 @@
     for rows in chunk_rows:
         acc[rows, :] = mm(local_t[:, rows], grid_ref[...], FIRST)
 
+    loaded("links")
+    links_col[...] = stand_up(links_ref)
+    early = mesh_rows // 2
+    count_into(counts, links_col, links_ref.shape[0], 0, early, 32)
+
     first = pl.ds(pl.multiple_of(mp * half, half), half)
     second = pl.ds(pl.multiple_of((1 - mp) * half, half), half)
 
@@ -226,30 +230,37 @@
     def widen(which, rows):
         return send(own.at[which, rows], other.at[which, rows], peer)
 
-    def mesh_block(which, wide, in_ref, out_ref, base_ref, dst_ref, after):
+    def mesh_block(which, pieces_of, wide, in_ref, out_ref, base_ref, dst_ref, after):
         parts = []
-        for rows, copy in zip(chunk_rows, wide):
-            copy.wait_recv()
+
+        def complete(c):
+            rows = pieces_of[c]
+            parts[c].wait_recv()
+            dst_ref[rows, :] = (
+                keep[rows, :] + part_in[which, rows, :].astype(jnp.float32)
+            ).astype(jnp.bfloat16)
+            after(rows)
+
+        for c, rows in enumerate(pieces_of):
+            wide[c].wait_recv()
             before = hidden_units(own[which, rows, :], other[which, rows, :], in_ref)[2]
             activated = (before * jax.nn.sigmoid(before)).astype(jnp.bfloat16)
             part_out[which, rows, :] = mm(activated, out_ref[:, second]).astype(jnp.bfloat16)
             parts.append(send(part_out.at[which, rows], part_in.at[which, rows], peer))
             keep[rows, :] = mm(activated, out_ref[:, first]) + base_ref[rows, :].astype(jnp.float32)
-        for rows, copy in zip(chunk_rows, parts):
-            copy.wait_recv()
-            dst_ref[rows, :] = (
-                keep[rows, :] + part_in[which, rows, :].astype(jnp.float32)
-            ).astype(jnp.bfloat16)
-            after(rows)
+            if c > 0:
+                complete(c - 1)
+        complete(len(pieces_of) - 1)
 
     for copy in slots:
         copy.wait_recv()
+    hop = 128
+    hop_rows = [pl.ds(c * hop, hop) for c in range(mesh_rows // hop)]
     wide = []
-    for rows in chunk_rows:
+    for rows in hop_rows:
         own[0, rows, :] = (mm(placer[rows, :], in_slots[...]) + acc[rows, :]).astype(jnp.bfloat16)
         wide.append(widen(0, rows))
 
-    hop = 128
     arriving = []
 
     def send_halo(rows):
@@ -262,11 +273,9 @@
                 arriving.append(send(state.at[part], halo.at[1, part], at(-1)))
 
     loaded("ein", "eout", "mesh")
-    mesh_block(0, wide, ein_ref, eout_ref, mesh_ref, state, send_halo)
-
-    loaded("links")
-    links_col[...] = stand_up(links_ref)
-    columns = links_ref.shape[0]
+    mesh_block(0, hop_rows, wide, ein_ref, eout_ref, mesh_ref, state, send_halo)
+
+    count_into(counts, links_col, links_ref.shape[0], early, mesh_rows - early, 32)
     steps = mesh_rows // hop
 
     def side_of(which):
@@ -278,7 +287,6 @@
 
     onward = []
     for k in range(steps):
-        count_into(counts, links_col, columns, k * hop, hop, 32)
         if grid_n == 2:
             part = pl.ds(k * hop, hop)
             arriving[k].wait_recv()
@@ -308,7 +316,7 @@
         ).astype(jnp.bfloat16)
         wide.append(widen(1, rows))
     loaded("pin", "pout", "din")
-    mesh_block(1, wide, pin_ref, pout_ref, state, final, lambda rows: None)
+    mesh_block(1, chunk_rows, wide, pin_ref, pout_ref, state, final, lambda rows: None)
 
     back_out[...] = mm(placer_rows[...], final[...]).astype(jnp.bfloat16)
     slots = []
@@ -330,8 +338,9 @@
         stage[rows, :] = values.astype(jnp.bfloat16)
 
     blocks = half // LANES
+    activated_t = jnp.transpose(activated)
     for side, cot in ((mp, cot_ref), (1 - mp, cot_other)):
-        down = mm(activated, cot[...], FIRST)
+        down = mm(activated_t, cot[...])
         for b in range(blocks):
             row = pl.multiple_of((side * blocks + b) * hidden, hidden)
             put(row, down[:, b * LANES : (b + 1) * LANES])
@@ -358,10 +367,6 @@
             put(row, up[:, b * LANES : (b + 1) * LANES])
     for i in range(ready, pieces):
         reduce_grid(i)
-
-    gpart_out[...] = mm(activated, dout_ref[:, second]).astype(jnp.bfloat16)
-    decoded = send(gpart_out, gpart_in, peer)
-    gkeep = mm(activated, dout_ref[:, first]) + grid_ref[...].astype(jnp.float32)
 
     mesh_sums = []
     for i in range(pieces):
@@ -379,8 +384,9 @@
             copies.append(send(stage_z.at[i, rows], rz.at[i, d - 1], along("mesh", mz, mesh_n, d)))
         mesh_sums.append(copies)
 
-    decoded.wait_recv()
-    pred_ref[...] = (gkeep + gpart_in[...].astype(jnp.float32)).astype(jnp.bfloat16)
+    gpart_out[...] = mm(activated, dout_ref[:, second]).astype(jnp.bfloat16)
+    decoded = send(gpart_out, gpart_in, peer)
+    gkeep = mm(activated, dout_ref[:, first]) + grid_ref[...].astype(jnp.float32)
 
     spread_mesh = []
     for i in range(pieces):
@@ -397,6 +403,9 @@
                 for d in range(1, mesh_n)
             ]
         )
+    decoded.wait_recv()
+    pred_ref[...] = (gkeep + gpart_in[...].astype(jnp.float32)).astype(jnp.bfloat16)
+
     spread_grid = []
     for i in range(pieces):
         for copy in spread_mesh[i]:
@@ -412,6 +421,19 @@
         copy.wait_send()
 
 
+def finish(pred_in, red_in, pred_ref, up_ref, down_ref):
+    pred_ref[...] = pred_in[...]
+    hidden, width = down_ref.shape
+    for b in range(width // LANES):
+        down_ref[:, b * LANES : (b + 1) * LANES] = red_in[b * hidden : (b + 1) * hidden, :].astype(
+            jnp.float32
+        )
+    start = width // LANES * hidden
+    for b in range(hidden // LANES):
+        rows = slice(start + b * width, start + (b + 1) * width)
+        up_ref[:, b * LANES : (b + 1) * LANES] = red_in[rows, :].astype(jnp.float32)
+
+
 def on_device(sizes, *args):
     mesh_n, grid_n = sizes
     grid_latent, mesh_latent, local_targets, grid_slots, mesh_slots, mesh_links = args[:6]
@@ -421,7 +443,7 @@
     width, hidden = weights[0].shape
     cap4 = grid_slots.size
     total, pieces, piece, by_grid, by_mesh = plan(mesh_n, grid_n, width, hidden)
-    copies = 4 + 1 + 4 + 4 + 4 * mesh_rows // 128 + 4 + 1 + 1 + 2 * pieces * (grid_n - 1 + mesh_n - 1)
+    copies = 4 + 1 + 8 + 4 + 4 + 4 * mesh_rows // 128 + 4 + 1 + 1 + 2 * pieces * (grid_n - 1 + mesh_n - 1)
     bf16, f32 = (jnp.bfloat16, jnp.float32)
     operands = (
         grid_latent,
@@ -479,16 +501,22 @@
         scratch_shapes=[pltpu.VMEM(shape, dtype) for shape, dtype in scratch]
         + [pltpu.SemaphoreType.DMA((n,)) for n in (copies, copies, len(operands))],
         compiler_params=pltpu.CompilerParams(
-            collective_id=0, has_side_effects=True, vmem_limit_bytes=40 * 1024 * 1024
+            collective_id=0, has_side_effects=True, vmem_limit_bytes=62 * 1024 * 1024
         ),
         name="forecast",
     )(*operands)
-    wide = reduced.astype(f32)
-    down = wide[: total // 2].reshape(width // LANES, hidden, LANES)
-    up = wide[total // 2 :].reshape(hidden // LANES, width, LANES)
-    grad_down = jnp.concatenate([down[b] for b in range(down.shape[0])], axis=1)
-    grad_up = jnp.concatenate([up[b] for b in range(up.shape[0])], axis=1)
-    return (prediction, grad_up, grad_down)
+    return pl.pallas_call(
+        finish,
+        out_shape=(
+            jax.ShapeDtypeStruct((grid_rows, half), bf16),
+            jax.ShapeDtypeStruct((width, hidden), f32),
+            jax.ShapeDtypeStruct((hidden, width), f32),
+        ),
+        in_specs=[vmem] * 2,
+        out_specs=(vmem,) * 3,
+        compiler_params=pltpu.CompilerParams(vmem_limit_bytes=62 * 1024 * 1024),
+        name="widen_grads",
+    )(prediction, reduced)
 
 
 def solution(mesh):

time: 71.1 us -> 60 us (0.84)
  local copies, waits for them, and re-layouts: 11.9 us -> 0 us
  Pallas kernels: 56.3 us -> 59.2 us
  other arithmetic: 1.66 us -> 0 us
    unnamed x27 -> x0, local copies, waits for them, and re-layouts: 11.9 us -> none
    pallas_call x0 -> x1, Pallas kernels: none -> 2.17 us  [on_device(): pl.pallas_call(finish, out_shape=(jax.ShapeDtypeStruct((grid_rows, half),...]
    concatenate x2 -> x0, other arithmetic: 1.66 us -> none  [the longest x1 0.83 us: on_device(): grad_down = jnp.concatenate([down[b] for b in range(down.shape[0])], axis=1)]
    pallas_call x1, Pallas kernels: 56.3 us -> 57 us  [on_device(): pl.pallas_call(functools.partial(kernel, sizes), out_shape=(jax.ShapeDtyp...]
where the time goes in v3:
time: 60 us; the launch traced here: 59.9 us
  Pallas kernels  59.2 us (99%)
  between operations  0.64 us (1%)
    pallas_call x1, Pallas kernels, on_device(): pl.pallas_call(functools.partial(kernel, sizes), out_shape=(jax.ShapeDtyp...  57 us
    pallas_call x1, Pallas kernels, on_device(): pl.pallas_call(finish, out_shape=(jax.ShapeDtypeStruct((grid_rows, half),...  2.17 us

profile of v3, /device:TPU:0, one launch (start us, length us, event | category | flops | bytes accessed | tf_op | source)
XLA Modules:
  0.0 59.9 jit_solution(3863711125910770067)
XLA Ops:
  0.6 57.0 %forecast.1 = (bf16[256,256]{1,0:T(8,128)(2,1)}, bf16[2048,128]{1,0:T(8,128)(2,1)}) custom-call(bf16[256,256]{1,0:T(8,128)(2,1)} %grid_hbm.1, bf16[512,256]{1,0:T(8,128)(2,1)} %mesh_hbm.1, s32[3,256]{1,0:T(4,128)} %bitcast.3, s32[4,32]{1,0:T(4,128)} %gslots_hbm.1, s32[4,32]{1,0:T(4,128)} %mslots_hbm.1, s32[6,512]{1,0:T(8,128)} %bitcast.2, ...), custom_call_target="tpu_custom_call" | custom-call | tf_op jit(solution)/shard_map/forecast/pallas_call | solution.py:493
  57.7 2.2 %widen_grads.1 = (bf16[256,256]{1,0:T(8,128)(2,1)}, f32[512,256]{1,0:T(8,128)}, f32[256,512]{1,0:T(8,128)}) custom-call(bf16[256,256]{1,0:T(8,128)(2,1)} %get-tuple-element.5.pred_in, bf16[2048,128]{1,0:T(8,128)(2,1)} %get-tuple-element.6.red_in), custom_call_target="tpu_custom_call" | custom-call | tf_op jit(solution)/shard_map/widen_grads/pallas_call | solution.py:508

commit v4 on v3

--- a/solution.py
+++ b/solution.py
@@ -209,8 +209,7 @@
 
     loaded("links")
     links_col[...] = stand_up(links_ref)
-    early = mesh_rows // 2
-    count_into(counts, links_col, links_ref.shape[0], 0, early, 32)
+    count_into(counts, links_col, links_ref.shape[0], 0, mesh_rows, 32)
 
     first = pl.ds(pl.multiple_of(mp * half, half), half)
     second = pl.ds(pl.multiple_of((1 - mp) * half, half), half)
@@ -275,7 +274,6 @@
     loaded("ein", "eout", "mesh")
     mesh_block(0, hop_rows, wide, ein_ref, eout_ref, mesh_ref, state, send_halo)
 
-    count_into(counts, links_col, links_ref.shape[0], early, mesh_rows - early, 32)
     steps = mesh_rows // hop
 
     def side_of(which):

time: 60 us -> 59.4 us (0.990)
  Pallas kernels: 59.2 us -> 58.6 us
where the time goes in v4:
time: 59.4 us; the launch traced here: 59.3 us
  Pallas kernels  58.6 us (99%)
  between operations  0.64 us (1%)
    pallas_call x1, Pallas kernels, on_device(): pl.pallas_call(functools.partial(kernel, sizes), out_shape=(jax.ShapeDtyp...  56.5 us
    pallas_call x1, Pallas kernels, on_device(): pl.pallas_call(finish, out_shape=(jax.ShapeDtypeStruct((grid_rows, half),...  2.17 us

profile of v4, /device:TPU:0, one launch (start us, length us, event | category | flops | bytes accessed | tf_op | source)
XLA Modules:
  0.0 59.3 jit_solution(7966765139064141165)
XLA Ops:
  0.6 56.5 %forecast.1 = (bf16[256,256]{1,0:T(8,128)(2,1)}, bf16[2048,128]{1,0:T(8,128)(2,1)}) custom-call(bf16[256,256]{1,0:T(8,128)(2,1)} %grid_hbm.1, bf16[512,256]{1,0:T(8,128)(2,1)} %mesh_hbm.1, s32[3,256]{1,0:T(4,128)} %bitcast.3, s32[4,32]{1,0:T(4,128)} %gslots_hbm.1, s32[4,32]{1,0:T(4,128)} %mslots_hbm.1, s32[6,512]{1,0:T(8,128)} %bitcast.2, ...), custom_call_target="tpu_custom_call" | custom-call | tf_op jit(solution)/shard_map/forecast/pallas_call | solution.py:491
  57.1 2.2 %widen_grads.1 = (bf16[256,256]{1,0:T(8,128)(2,1)}, f32[512,256]{1,0:T(8,128)}, f32[256,512]{1,0:T(8,128)}) custom-call(bf16[256,256]{1,0:T(8,128)(2,1)} %get-tuple-element.5.pred_in, bf16[2048,128]{1,0:T(8,128)(2,1)} %get-tuple-element.6.red_in), custom_call_target="tpu_custom_call" | custom-call | tf_op jit(solution)/shard_map/widen_grads/pallas_call | solution.py:506
